TPU v7x, 32 devices: a whole 2x2x4 slice. The times are simulated.
32 devices in a mesh: grp: 2 (over y), lon: 2 (over x), lat: 4 (over z), lev: 2 (over core).
Axes of the slice: x: 2, y: 2, z: 4, core: 2. Of those that a mesh axis runs over, the one named last changes fastest.
Arguments:
- state: bfloat16 [16, 8, 96, 4, 256], P(('grp', 'lat'), 'lon', 'lev'), parts along dimension 0, may hold values from -6 to 6
- adj_in: bfloat16 [16, 8, 2, 96, 4, 128], P(('grp', 'lat'), 'lon', None, 'lev'), parts along dimension 0, may hold values from -6 to 6
- weights: bfloat16 [16, 8, 2, 128, 256], P(('grp', 'lat'), 'lon'), parts along dimension 0, may hold values from -0.5 to 0.5
- slopes: bfloat16 [16, 8, 2, 128, 256], P(('grp', 'lat'), 'lon'), parts along dimension 0, may hold values from -0.01953125 to 0.01953125
- dep_lat: int32 [16, 8, 2], P(('grp', 'lat'), 'lon'), parts along dimension 0, may hold values from -2 to 2, as said below
- dep_lon: int32 [16, 8, 2], P(('grp', 'lat'), 'lon'), parts along dimension 0, may hold values from -2 to 2, as said below
Outputs:
- src_adj: float32 [16, 8, 96, 4, 256], P(('grp', 'lat'), 'lon', 'lev'), parts along dimension 0
- wind_adj: float32 [16, 8, 2, 128], P(('grp', 'lat'), 'lon'), parts along dimension 0
There are 2 independent parts, one for each index of `grp`. A program takes and returns all parts, laid end to end along the dimension named above; each array names one. Nothing has to cross between parts.
Inputs may be any that keep to these rules, and one draw needn't show every extreme that they name: row + dep_lat stays within 0 to 7. |dep_lon| is at most 2 in the rows of the first and last quarter of latitudes and at most 1 elsewhere; longitude wraps around.
All inputs are finite; a program needn't handle non-finite values.
Results may differ from a plain program's by a relative error of at most 0.0003.
Values may be sent and summed in bfloat16 or wider, within the bound.
A program may use at most 64 MiB of HBM per device.

v0:
```python
import jax
import jax.numpy as jnp
from jax import lax
from jax.sharding import PartitionSpec as P

HW = 2


def with_halo(array, sides, width, wrap):
    for axis, dim in sides:
        peers, length = (lax.axis_size(axis), array.shape[dim])
        up = [(i, (i + 1) % peers) for i in range(peers if wrap else peers - 1)]
        down = [(j, i) for i, j in up]
        last = lax.slice_in_dim(array, length - width, length, axis=dim)
        initial = lax.slice_in_dim(array, 0, width, axis=dim)
        before = lax.ppermute(last, axis, up)
        after = lax.ppermute(initial, axis, down)
        array = jnp.concatenate([before, array, after], axis=dim)
    return array


def fold_lon(buffer):
    rims = jnp.concatenate([buffer[:, :HW], buffer[:, -HW:]], axis=1)
    got = with_halo(rims, (("lon", 1),), HW, True)
    middle = buffer[:, HW:-HW]
    middle = middle.at[:, :HW].add(got[:, :HW])
    middle = middle.at[:, -HW:].add(got[:, -HW:])
    return middle


def fold_lat(buffer):
    rims = jnp.concatenate([buffer[:HW], buffer[-HW:]], axis=0)
    got = with_halo(rims, (("lat", 0),), HW, False)
    middle = buffer[HW:-HW]
    middle = middle.at[:HW].add(got[:HW])
    middle = middle.at[-HW:].add(got[-HW:])
    return middle


def on_device(state, adj_in, weights, slopes, dep_lat, dep_lon):
    rows_dev, cols_dev, levels_dev, fields, cells = state.shape
    tiles_blk = adj_in.shape[2]
    points = adj_in.shape[-1]
    channels = levels_dev * fields
    ntile = rows_dev * cols_dev * tiles_blk
    tall = rows_dev + 2 * HW
    wide = cols_dev + 2 * HW
    extended = with_halo(state, (("lat", 0), ("lon", 1)), HW, True)
    blocks = extended.reshape(tall * wide, channels, cells)
    row_ids = jnp.arange(rows_dev, dtype=jnp.int32)[:, None, None]
    col_ids = jnp.arange(cols_dev, dtype=jnp.int32)[None, :, None]
    target = ((row_ids + HW + dep_lat) * wide + col_ids + HW + dep_lon).reshape(ntile)
    picked = blocks[target]
    slope_flat = slopes.reshape(ntile, points, cells)
    weight_flat = weights.reshape(ntile, points, cells)
    adj_flat = adj_in.reshape(ntile, channels, points)
    deriv = jnp.einsum("tpc,tmc->tmp", slope_flat, picked, preferred_element_type=jnp.float32)
    partial_wind = jnp.sum(deriv * adj_flat.astype(jnp.float32), axis=1)
    wind = lax.psum(partial_wind, "lev")
    wind_adj = wind.reshape(rows_dev, cols_dev, tiles_blk, points)
    contrib = jnp.einsum("tmp,tpc->tmc", adj_flat, weight_flat, preferred_element_type=jnp.float32)
    summed = jax.ops.segment_sum(
        contrib.reshape(ntile, channels * cells), target, num_segments=tall * wide
    )
    summed = summed.reshape(tall, wide, channels, cells)
    owned = fold_lat(fold_lon(summed))
    src_adj = owned.reshape(rows_dev, cols_dev, levels_dev, fields, cells)
    return (src_adj, wind_adj)


def solution(mesh):
    placed = (
        P(("grp", "lat"), "lon", "lev", None, None),
        P(("grp", "lat"), "lon", None, "lev", None, None),
        P(("grp", "lat"), "lon", None, None, None),
        P(("grp", "lat"), "lon", None, None, None),
        P(("grp", "lat"), "lon", None),
        P(("grp", "lat"), "lon", None),
    )
    return jax.shard_map(
        on_device,
        mesh=mesh,
        in_specs=placed,
        out_specs=(
            P(("grp", "lat"), "lon", "lev", None, None),
            P(("grp", "lat"), "lon", None, None),
        ),
        check_vma=False,
    )
```

profile of v0, /device:TPU:0, one launch (start us, length us, event | category | flops | bytes accessed | tf_op | source)
XLA Modules:
  0.0 205.6 jit_solution(9640086704920432461)
XLA Ops:
  0.6 0.0 copy-start
  0.7 1.2 copy-done
  1.9 1.7 fusion.9
  3.6 0.0 copy-start.5
  3.6 0.0 copy-start.6
  3.6 3.5 %copy.12 = f32[2,8,192,256]{3,1,2,0:T(8,128)} copy(f32[2,8,192,256]{3,2,1,0:T(8,128)S(1)} %bitcast.21) | data formatting | bytes 6291456
  7.1 0.0 copy-done.5
  7.1 0.1 add_add_fusion
  7.1 0.1 copy.10
  7.2 0.1 reshape.224
  7.3 9.4 %scatter_custom_fusion = f32[48,49152]{1,0:T(8,128)} fusion(s32[16]{0:T(128)S(1)} %reshape.224, f32[16,49152]{1,0:T(8,128)} %bitcast.22, f32[]{:T(128)} %constant.126.clone.1), kind=kCustom, calls=%fused_computation.4 | custom fusion | flops 786432 | bytes 9437696 | tf_op jit(solution)/shard_map/scatter-add | solution.py:62
  16.8 6.6 %copy.15 = f32[6,8,192,256]{3,2,1,0:T(8,128)S(1)} copy(f32[6,8,192,256]{3,1,2,0:T(8,128)} %bitcast.20) | data formatting | bytes 18874368
  23.4 0.0 copy-start.4
  23.4 0.5 fusion.6
  23.9 3.0 %collective-permute-start = (f32[6,2,192,256]{3,2,1,0:T(8,128)S(1)}, f32[6,2,192,256]{3,2,1,0:T(8,128)S(1)}, u32[]{:S(2)}, u32[]{:S(2)}) collective-permute-start(f32[6,2,192,256]{3,2,1,0:T(8,128)S(1)} %get-tuple-element.67), channel_id=1, source_target_pairs={{0,8},{8,0},{1,9},{9,1},{2,10},{10,2},{3,11},{11,3},{4,12},{12,4},... | collective-permute-start | bytes 7077896 | tf_op jit(solution)/shard_map/ppermute | solution.py:16
  26.9 0.1 collective-permute-start.1
  27.0 0.0 copy-done.4
  27.0 2.0 collective-permute-start.4
  29.0 2.0 collective-permute-start.5
  31.0 0.4 slice.143
  31.5 18.0 %collective-permute-done.4 = bf16[2,4,48,4,256]{4,3,2,1,0:T(4,128)(2,1)S(1)} collective-permute-done((bf16[2,4,48,4,256]{4,3,2,1,0:T(4,128)(2,1)S(1)}, bf16[2,4,48,4,256]{4,3,2,1,0:T(4,128)(2,1)S(1)}, u32[]{:S(2)}, u32[]{:S(2)}) %collective-permute-start.4) | collective-permute-done | bytes 786464 | tf_op jit(solution)/shard_map/ppermute | solution.py:16
  49.5 0.3 constant_dynamic-update-slice_fusion.2
  49.8 0.3 constant_dynamic-update-slice_fusion.1
  50.1 14.2 %collective-permute-done.5 = bf16[2,4,48,4,256]{4,3,2,1,0:T(4,128)(2,1)S(1)} collective-permute-done((bf16[2,4,48,4,256]{4,3,2,1,0:T(4,128)(2,1)S(1)}, bf16[2,4,48,4,256]{4,3,2,1,0:T(4,128)(2,1)S(1)}, u32[]{:S(2)}, u32[]{:S(2)}) %collective-permute-start.5) | collective-permute-done | bytes 786464 | tf_op jit(solution)/shard_map/ppermute | solution.py:17
  64.3 0.4 constant_dynamic-update-slice_fusion
  64.6 2.5 %fusion.8 = (bf16[6,2,48,4,256]{4,3,2,1,0:T(4,128)(2,1)}, bf16[6,2,48,4,256]{4,3,2,1,0:T(4,128)(2,1)}) fusion(bf16[6,4,48,4,256]{4,3,2,1,0:T(4,128)(2,1)S(1)} %constant_dynamic-update-slice_fusion), kind=kLoop, calls=%fused_computation.23 | loop fusion | bytes 4718592 | tf_op jit(solution)/shard_map/slice | solution.py:14
  67.1 1.5 collective-permute-start.6
  68.6 0.5 collective-permute-start.7
  69.2 9.8 %collective-permute-done = f32[6,2,192,256]{3,2,1,0:T(8,128)S(1)} collective-permute-done((f32[6,2,192,256]{3,2,1,0:T(8,128)S(1)}, f32[6,2,192,256]{3,2,1,0:T(8,128)S(1)}, u32[]{:S(2)}, u32[]{:S(2)}) %collective-permute-start) | collective-permute-done | bytes 2359328 | tf_op jit(solution)/shard_map/ppermute | solution.py:16
  79.0 0.4 fusion.3
  79.4 50.1 %collective-permute-done.1 = f32[6,2,192,256]{3,2,1,0:T(8,128)S(1)} collective-permute-done((f32[6,2,192,256]{3,2,1,0:T(8,128)S(1)}, f32[6,2,192,256]{3,2,1,0:T(8,128)S(1)}, u32[]{:S(2)}, u32[]{:S(2)}) %collective-permute-start.1) | collective-permute-done | bytes 2359328 | tf_op jit(solution)/shard_map/ppermute | solution.py:17
  129.5 0.6 fusion.2
  130.1 2.3 %fusion.7 = (f32[2,4,192,256]{3,2,1,0:T(8,128)}, f32[2,4,192,256]{3,2,1,0:T(8,128)}) fusion(f32[6,4,192,256]{3,2,1,0:T(8,128)S(1)} %fusion.2), kind=kLoop, calls=%fused_computation.22 | loop fusion | bytes 6291456 | tf_op jit(solution)/shard_map/slice | solution.py:32
  132.4 1.0 copy-done.2
  133.4 5.2 %collective-permute-start.2 = (f32[2,4,192,256]{3,2,1,0:T(8,128)}, f32[2,4,192,256]{3,2,1,0:T(8,128)}, u32[]{:S(2)}, u32[]{:S(2)}) collective-permute-start(f32[2,4,192,256]{3,2,1,0:T(8,128)} %get-tuple-element.68), channel_id=1, source_target_pairs={{0,2},{2,4},{4,6},{1,3},{3,5},{5,7},{8,10},{10,12},{12,14},{9,11},... | collective-permute-start | bytes 4718600 | tf_op jit(solution)/shard_map/ppermute | solution.py:16
  138.6 1.3 collective-permute-start.3
  139.9 0.1 broadcast_in_dim_reshape.3
  140.0 14.9 %collective-permute-done.6 = bf16[6,2,48,4,256]{4,3,2,1,0:T(4,128)(2,1)} collective-permute-done((bf16[6,2,48,4,256]{4,3,2,1,0:T(4,128)(2,1)}, bf16[6,2,48,4,256]{4,3,2,1,0:T(4,128)(2,1)}, u32[]{:S(2)}, u32[]{:S(2)}) %collective-permute-start.6) | collective-permute-done | bytes 1179680 | tf_op jit(solution)/shard_map/ppermute | solution.py:16
  154.9 24.4 %collective-permute-done.7 = bf16[6,2,48,4,256]{4,3,2,1,0:T(4,128)(2,1)} collective-permute-done((bf16[6,2,48,4,256]{4,3,2,1,0:T(4,128)(2,1)}, bf16[6,2,48,4,256]{4,3,2,1,0:T(4,128)(2,1)}, u32[]{:S(2)}, u32[]{:S(2)}) %collective-permute-start.7) | collective-permute-done | bytes 1179680 | tf_op jit(solution)/shard_map/ppermute | solution.py:17
  179.3 6.2 %pad_maximum_fusion = bf16[6,8,48,4,256]{4,3,2,1,0:T(4,128)(2,1)} fusion(bf16[6,2,48,4,256]{4,3,2,1,0:T(4,128)(2,1)} %collective-permute-done.7, bf16[6,4,48,4,256]{4,3,2,1,0:T(4,128)(2,1)S(1)} %constant_dynamic-update-slice_fusion, bf16[6,2,48,4,256]{4,3,2,1,0:T(4,128)(2,1)} %collective-permute-done.6), kind=kLoop, calls=%fused_computation.3 | loop fusion | flops 4718592 | bytes 9437184 | tf_op jit(solution)/shard_map/concatenate | solution.py:18
  185.5 7.7 %reshape.211 = bf16[48,192,256]{2,1,0:T(8,128)(2,1)} reshape(bf16[6,8,48,4,256]{4,3,2,1,0:T(4,128)(2,1)} %pad_maximum_fusion) | data formatting | bytes 9437184 | tf_op jit(solution)/shard_map/reshape | solution.py:49
  193.2 3.1 %gather_fusion = bf16[16,192,256]{2,1,0:T(8,128)(2,1)S(1)} fusion(bf16[48,192,256]{2,1,0:T(8,128)(2,1)} %reshape.211, s32[1024]{0:T(1024)S(1)} %pad_clamp_fusion), kind=kCustom, calls=%fused_computation | custom fusion | bytes 3145792 | tf_op jit(solution)/shard_map/gather | solution.py:53
  196.3 1.8 multiply_reduce_fusion
  198.1 3.1 %psum.7 = f32[2,4,2,128]{3,2,1,0:T(2,128)} all-reduce(f32[2,4,2,128]{3,2,1,0:T(2,128)S(1)} %bitcast.25), channel_id=1, replica_groups=mesh['grp'=2,'lon'=2,'lat'=4,'lev'=2] {'lev'}, use_global_device_ids=true, to_apply=%region_2.0 | all-reduce | flops 2048 | bytes 16384 | tf_op jit(solution)/shard_map/psum | solution.py:59
  201.2 0.0 collective-permute-done.2
  201.2 0.0 collective-permute-done.3
  201.2 2.8 %fusion.4 = f32[2,4,192,256]{3,2,1,0:T(8,128)S(1)} fusion(f32[2,4,192,256]{3,2,1,0:T(8,128)} %collective-permute-done.3, f32[2,4,192,256]{3,2,1,0:T(8,128)} %collective-permute-done.2, f32[6,4,192,256]{3,2,1,0:T(8,128)} %copy-done.2), kind=kLoop, calls=%fused_computation.11 | loop fusion | flops 786432 | bytes 6291456 | tf_op jit(solution)/shard_map/add | solution.py:36
  204.0 1.6 reshape.210
  (9 shorter events, 0.0 us)
Async XLA Ops:
  0.6 1.2 copy-start
  3.6 3.5 %copy-start.5 = (s32[2,4,2]{1,2,0:T(2,128)S(1)}, s32[2,4,2]{1,2,0:T(2,128)}, u32[]{:S(2)}) copy-start(s32[2,4,2]{1,2,0:T(2,128)} %param.23) | copy-start | bytes 196
  3.6 3.5 %copy-start.6 = (s32[2,4,2]{1,2,0:T(2,128)S(1)}, s32[2,4,2]{1,2,0:T(2,128)}, u32[]{:S(2)}) copy-start(s32[2,4,2]{1,2,0:T(2,128)} %param.22) | copy-start | bytes 196
  23.4 3.6 %copy-start.4 = (bf16[2,4,48,4,256]{4,3,2,1,0:T(4,128)(2,1)S(1)}, bf16[2,4,48,4,256]{4,3,2,1,0:T(4,128)(2,1)}, u32[]{:S(2)}) copy-start(bf16[2,4,48,4,256]{4,3,2,1,0:T(4,128)(2,1)} %param.18) | copy-start | bytes 2359300
  23.9 55.1 %collective-permute-start = (f32[6,2,192,256]{3,2,1,0:T(8,128)S(1)}, f32[6,2,192,256]{3,2,1,0:T(8,128)S(1)}, u32[]{:S(2)}, u32[]{:S(2)}) collective-permute-start(f32[6,2,192,256]{3,2,1,0:T(8,128)S(1)} %get-tuple-element.67), channel_id=1, source_target_pairs={{0,8},{8,0},{1,9},{9,1},{2,10},{10,2},{3,11},{11,3},{4,12},{12,4},... | collective-permute-start | bytes 7077896 | tf_op jit(solution)/shard_map/ppermute | solution.py:16
  26.9 102.6 %collective-permute-start.1 = (f32[6,2,192,256]{3,2,1,0:T(8,128)S(1)}, f32[6,2,192,256]{3,2,1,0:T(8,128)S(1)}, u32[]{:S(2)}, u32[]{:S(2)}) collective-permute-start(f32[6,2,192,256]{3,2,1,0:T(8,128)S(1)} %get-tuple-element.66), channel_id=1, source_target_pairs={{8,0},{0,8},{9,1},{1,9},{10,2},{2,10},{11,3},{3,11},{12,4},{4,12},... | collective-permute-start | bytes 7077896 | tf_op jit(solution)/shard_map/ppermute | solution.py:17
  27.0 22.5 %collective-permute-start.4 = (bf16[2,4,48,4,256]{4,3,2,1,0:T(4,128)(2,1)S(1)}, bf16[2,4,48,4,256]{4,3,2,1,0:T(4,128)(2,1)S(1)}, u32[]{:S(2)}, u32[]{:S(2)}) collective-permute-start(bf16[2,4,48,4,256]{4,3,2,1,0:T(4,128)(2,1)S(1)} %copy-done.4), channel_id=1, source_target_pairs={{0,2},{2,4},{4,6},{6,0},{1,3},{3,5},{5,7},{7,1},{8,10},{10,12},{12... | collective-permute-start | bytes 2359304 | tf_op jit(solution)/shard_map/ppermute | solution.py:16
  29.0 35.3 %collective-permute-start.5 = (bf16[2,4,48,4,256]{4,3,2,1,0:T(4,128)(2,1)S(1)}, bf16[2,4,48,4,256]{4,3,2,1,0:T(4,128)(2,1)S(1)}, u32[]{:S(2)}, u32[]{:S(2)}) collective-permute-start(bf16[2,4,48,4,256]{4,3,2,1,0:T(4,128)(2,1)S(1)} %copy-done.4), channel_id=1, source_target_pairs={{2,0},{4,2},{6,4},{0,6},{3,1},{5,3},{7,5},{1,7},{10,8},{12,10},{14... | collective-permute-start | bytes 2359304 | tf_op jit(solution)/shard_map/ppermute | solution.py:17
  67.1 87.8 %collective-permute-start.6 = (bf16[6,2,48,4,256]{4,3,2,1,0:T(4,128)(2,1)}, bf16[6,2,48,4,256]{4,3,2,1,0:T(4,128)(2,1)}, u32[]{:S(2)}, u32[]{:S(2)}) collective-permute-start(bf16[6,2,48,4,256]{4,3,2,1,0:T(4,128)(2,1)} %get-tuple-element.70), channel_id=1, source_target_pairs={{0,8},{8,0},{1,9},{9,1},{2,10},{10,2},{3,11},{11,3},{4,12},{12,4},... | collective-permute-start | bytes 3538952 | tf_op jit(solution)/shard_map/ppermute | solution.py:16
  68.6 110.7 %collective-permute-start.7 = (bf16[6,2,48,4,256]{4,3,2,1,0:T(4,128)(2,1)}, bf16[6,2,48,4,256]{4,3,2,1,0:T(4,128)(2,1)}, u32[]{:S(2)}, u32[]{:S(2)}) collective-permute-start(bf16[6,2,48,4,256]{4,3,2,1,0:T(4,128)(2,1)} %get-tuple-element.71), channel_id=1, source_target_pairs={{8,0},{0,8},{9,1},{1,9},{10,2},{2,10},{11,3},{3,11},{12,4},{4,12},... | collective-permute-start | bytes 3538952 | tf_op jit(solution)/shard_map/ppermute | solution.py:17
  130.1 3.3 %copy-start.2 = (f32[6,4,192,256]{3,2,1,0:T(8,128)}, f32[6,4,192,256]{3,2,1,0:T(8,128)S(1)}, u32[]{:S(2)}) copy-start(f32[6,4,192,256]{3,2,1,0:T(8,128)S(1)} %fusion.2) | copy-start | bytes 14155780
  133.4 67.8 %collective-permute-start.2 = (f32[2,4,192,256]{3,2,1,0:T(8,128)}, f32[2,4,192,256]{3,2,1,0:T(8,128)}, u32[]{:S(2)}, u32[]{:S(2)}) collective-permute-start(f32[2,4,192,256]{3,2,1,0:T(8,128)} %get-tuple-element.68), channel_id=1, source_target_pairs={{0,2},{2,4},{4,6},{1,3},{3,5},{5,7},{8,10},{10,12},{12,14},{9,11},... | collective-permute-start | bytes 4718600 | tf_op jit(solution)/shard_map/ppermute | solution.py:16
  138.6 62.6 %collective-permute-start.3 = (f32[2,4,192,256]{3,2,1,0:T(8,128)}, f32[2,4,192,256]{3,2,1,0:T(8,128)}, u32[]{:S(2)}, u32[]{:S(2)}) collective-permute-start(f32[2,4,192,256]{3,2,1,0:T(8,128)} %get-tuple-element.69), channel_id=1, source_target_pairs={{2,0},{4,2},{6,4},{3,1},{5,3},{7,5},{10,8},{12,10},{14,12},{11,9},... | collective-permute-start | bytes 4718600 | tf_op jit(solution)/shard_map/ppermute | solution.py:17
  193.2 3.1 %copy-start.3 = (bf16[2,4,2,48,4,128]{5,4,3,2,1,0:T(4,128)(2,1)S(1)}, bf16[2,4,2,48,4,128]{5,4,3,2,1,0:T(4,128)(2,1)}, u32[]{:S(2)}) copy-start(bf16[2,4,2,48,4,128]{5,4,3,2,1,0:T(4,128)(2,1)} %param.19) | copy-start | bytes 2359300
  201.2 4.4 %copy-start.1 = (bf16[2,4,2,128,256]{4,3,2,1,0:T(8,128)(2,1)S(1)}, bf16[2,4,2,128,256]{4,3,2,1,0:T(8,128)(2,1)}, u32[]{:S(2)}) copy-start(bf16[2,4,2,128,256]{4,3,2,1,0:T(8,128)(2,1)} %param.20) | copy-start | bytes 3145732
where the time goes:
time: 206 us
  waiting for transfers between devices  131 us (64%)
  local copies, waits for them, and re-layouts  31.6 us (15%)
  other arithmetic  19.6 us (10%)
  starting transfers between devices  15.6 us (8%)
  matrix products  3.49 us (2%)
  blocking collectives  3.09 us (2%)
    ppermute x4, waiting for transfers between devices, with_halo(): after = lax.ppermute(initial, axis, down)  88.7 us
    ppermute x4, waiting for transfers between devices, with_halo(): before = lax.ppermute(last, axis, up)  42.7 us
    unnamed x18, local copies, waits for them, and re-layouts  13 us
    ppermute x4, starting transfers between devices, with_halo(): before = lax.ppermute(last, axis, up)  11.7 us
    scatter-add x1, other arithmetic, on_device(): jax.ops.segment_sum(contrib.reshape(ntile, channels * cells), target, num...  9.43 us
    reshape x1, local copies, waits for them, and re-layouts, on_device(): blocks = extended.reshape(tall * wide, channels, cells)  7.7 us
    concatenate x1, other arithmetic, with_halo(): array = jnp.concatenate([before, array, after], axis=dim)  6.17 us
  transfers between devices with their start and end apart: 8, of which 6 were waited for; matrix products, arithmetic and copies ran while one was open for 13% of the time, Pallas kernels for 0%

commit v1 on v0

--- a/solution.py
+++ b/solution.py
@@ -1,9 +1,15 @@
+import functools
+
 import jax
 import jax.numpy as jnp
 from jax import lax
+from jax.experimental import pallas as pl
+from jax.experimental.pallas import tpu as pltpu
 from jax.sharding import PartitionSpec as P
 
 HW = 2
+MESH = pl.DeviceIdType.MESH
+REGION = 16
 
 
 def with_halo(array, sides, width, wrap):
@@ -37,7 +43,7 @@
     return middle
 
 
-def on_device(state, adj_in, weights, slopes, dep_lat, dep_lon):
+def halo_path(state, adj_in, weights, slopes, dep_lat, dep_lon):
     rows_dev, cols_dev, levels_dev, fields, cells = state.shape
     tiles_blk = adj_in.shape[2]
     points = adj_in.shape[-1]
@@ -57,15 +63,430 @@
     deriv = jnp.einsum("tpc,tmc->tmp", slope_flat, picked, preferred_element_type=jnp.float32)
     partial_wind = jnp.sum(deriv * adj_flat.astype(jnp.float32), axis=1)
     wind = lax.psum(partial_wind, "lev")
-    wind_adj = wind.reshape(rows_dev, cols_dev, tiles_blk, points)
     contrib = jnp.einsum("tmp,tpc->tmc", adj_flat, weight_flat, preferred_element_type=jnp.float32)
     summed = jax.ops.segment_sum(
         contrib.reshape(ntile, channels * cells), target, num_segments=tall * wide
     )
     summed = summed.reshape(tall, wide, channels, cells)
     owned = fold_lat(fold_lon(summed))
-    src_adj = owned.reshape(rows_dev, cols_dev, levels_dev, fields, cells)
-    return (src_adj, wind_adj)
+    return owned.reshape(rows_dev * cols_dev, channels, cells), wind
+
+
+class Plan:
+    def __init__(self, mesh, ntile):
+        self.nlat, self.nlon = mesh.shape["lat"], mesh.shape["lon"]
+        lons = (0, 1) if self.nlon == 2 else (0, 1, -1)
+        self.near = [(a, b) for b in lons for a in (-1, 1, 0) if (a, b) != (0, 0)]
+        self.near.sort(key=lambda d: -(abs(d[0]) + abs(d[1])))
+        self.caps, self.bases, self.chunks = [], [], []
+        for a, b in self.near:
+            cap = 5 if a and b else (8 if b else 9)
+            self.bases.append(sum(self.caps))
+            self.caps.append(cap)
+            self.chunks.append([(0, 4, False), (4, 4, True)] if b and not a else [(0, cap, False)])
+        self.slots = sum(self.caps)
+        self.count = len(self.near)
+
+    def polar(self, lat):
+        quarter = max(self.nlat // 4, 1)
+        return (lat < quarter) | (lat >= self.nlat - quarter)
+
+    def exists(self, lat, step):
+        if step == 0:
+            return lat >= 0
+        return (lat + step >= 0) & (lat + step < self.nlat)
+
+    def device(self, step, sign=1, core=None):
+        a, b = step
+        lat = lax.axis_index("lat") + sign * a
+        lon = lax.rem(lax.axis_index("lon") + sign * b + self.nlon, self.nlon)
+        core = lax.axis_index("lev") if core is None else core
+        return (lax.axis_index("grp"), lon, lat, core)
+
+
+def index_of_axes(mesh, named):
+    order = {"grp": 0, "lon": 1, "lat": 2, "lev": 3}
+    return tuple(named[order[a]] for a in mesh.axis_names)
+
+
+def pack_kernel(
+    plan, dims, dlat, dlon, adj, wts, slp, padj, pwts, pslp, dest, own, slot, over, fill, sems
+):
+    rows, cols, tpb, half = dims
+    lat, core = lax.axis_index("lat"), lax.axis_index("lev")
+    for k in range(plan.count):
+        fill[k] = 0
+        for s in range(REGION):
+            dest[k, s] = -1
+    over[0] = 0
+    ntile = rows * cols * tpb
+
+    def copies(t, at):
+        rowsl = pl.ds(pl.multiple_of(core * half, half), half)
+        return [
+            pltpu.make_async_copy(wts.at[t, rowsl], pwts.at[at], sems.at[t, 0]),
+            pltpu.make_async_copy(slp.at[t, rowsl], pslp.at[at], sems.at[t, 1]),
+            pltpu.make_async_copy(adj.at[t], padj.at[at], sems.at[t, 2]),
+        ]
+
+    def place(t, _):
+        r = t // (cols * tpb)
+        c = lax.rem(t // tpb, cols)
+        sr, sc = r + dlat[t], c + dlon[t]
+        a = jnp.where(sr < 0, -1, jnp.where(sr >= rows, 1, 0))
+        b = jnp.where(sc < 0, -1, jnp.where(sc >= cols, 1, 0))
+        block = (sr - a * rows) * cols + sc - b * cols
+        if plan.nlon == 2:
+            b = jnp.abs(b)
+        home = (a == 0) & (b == 0)
+        own[t] = jnp.where(home, block, -1)
+
+        @pl.when(home)
+        def _():
+            slot[t] = plan.count * REGION + t
+            fill[plan.count + t] = -1
+
+        for k, (x, y) in enumerate(plan.near):
+
+            @pl.when((a == x) & (b == y))
+            def _(k=k, x=x, y=y):
+                pos = fill[k]
+                fill[k] = pos + 1
+                room = plan.caps[k]
+                if y and not x:
+                    room = jnp.where(plan.polar(lat), room, 4)
+                fits = pos < room
+                at = jnp.where(fits, pos, 0)
+                slot[t] = k * REGION + at
+                fill[plan.count + t] = jnp.where(fits, plan.bases[k] + at, -1)
+
+                @pl.when(fits)
+                def _():
+                    dest[k, at] = block
+                    for copy in copies(t, plan.bases[k] + at):
+                        copy.start()
+
+                @pl.when(~fits)
+                def _():
+                    over[0] = 1
+
+        return 0
+
+    lax.fori_loop(0, ntile, place, 0)
+
+    def finish(t, _):
+        at = fill[plan.count + t]
+
+        @pl.when(at >= 0)
+        def _():
+            for copy in copies(t, at):
+                copy.wait()
+
+        return 0
+
+    lax.fori_loop(0, ntile, finish, 0)
+
+
+def send_kernel(
+    plan, mesh, padj, pwts, pslp, pdest, radj, rwts, rslp, rdest, ssem, rsem, fsem, gsem
+):
+    lat, core = lax.axis_index("lat"), lax.axis_index("lev")
+    polar = plan.polar(lat)
+    partner = index_of_axes(
+        mesh, (lax.axis_index("grp"), lax.axis_index("lon"), lat, 1 - core)
+    )
+    barrier = pltpu.get_barrier_semaphore()
+    expected = 1
+    pl.semaphore_signal(barrier, inc=1, device_id=partner, device_id_type=MESH)
+    for step in plan.near:
+        there = plan.exists(lat, step[0])
+        expected = expected + there.astype(jnp.int32)
+
+        @pl.when(there)
+        def _(step=step):
+            pl.semaphore_signal(
+                barrier, inc=1, device_id=index_of_axes(mesh, plan.device(step)), device_id_type=MESH
+            )
+
+    pl.semaphore_wait(barrier, expected)
+
+    def groups():
+        n = 0
+        for k, step in enumerate(plan.near):
+            for off, size, far in plan.chunks[k]:
+                rows = pl.ds(plan.bases[k] + off, size)
+                send, get = plan.exists(lat, step[0]), plan.exists(lat, -step[0])
+                if far:
+                    send, get = send & polar, get & polar
+                yield n, k, step, off, rows, send, get
+                n += 1
+
+    def outgoing(n, step, rows):
+        device = index_of_axes(mesh, plan.device(step))
+        pairs = [
+            (pwts.at[rows], rwts.at[rows, core]),
+            (pslp.at[rows], rslp.at[rows, core]),
+            (padj.at[rows], radj.at[rows]),
+        ]
+        return [
+            pltpu.make_async_remote_copy(
+                src_ref=src, dst_ref=dst, send_sem=ssem.at[n, j], recv_sem=rsem.at[n, j],
+                device_id=device, device_id_type=MESH,
+            )
+            for j, (src, dst) in enumerate(pairs)
+        ]
+
+    def table(k, step):
+        return pltpu.make_async_remote_copy(
+            src_ref=pdest.at[k], dst_ref=rdest.at[k],
+            send_sem=ssem.at[plan.copies + k, 0], recv_sem=rsem.at[plan.copies + k, 0],
+            device_id=index_of_axes(mesh, plan.device(step)), device_id_type=MESH,
+        )
+
+    def passed(n, rows):
+        return [
+            pltpu.make_async_remote_copy(
+                src_ref=ref.at[rows, core], dst_ref=ref.at[rows, core],
+                send_sem=fsem.at[n, j], recv_sem=gsem.at[n, j],
+                device_id=partner, device_id_type=MESH,
+            )
+            for j, ref in enumerate((rwts, rslp))
+        ]
+
+    for n, k, step, off, rows, send, get in groups():
+
+        @pl.when(send)
+        def _():
+            if off == 0:
+                table(k, step).start()
+            for copy in outgoing(n, step, rows):
+                copy.start()
+
+    for n, k, step, off, rows, send, get in groups():
+
+        @pl.when(get)
+        def _():
+            arrive, on = outgoing(n, step, rows), passed(n, rows)
+            for j in range(2):
+                arrive[j].wait_recv()
+                on[j].start()
+
+    for n, k, step, off, rows, send, get in groups():
+
+        @pl.when(get)
+        def _():
+            if off == 0:
+                table(k, step).wait_recv()
+            outgoing(n, step, rows)[2].wait_recv()
+            for copy in passed(n, rows):
+                copy.wait()
+
+        @pl.when(send)
+        def _():
+            if off == 0:
+                table(k, step).wait_send()
+            for copy in outgoing(n, step, rows):
+                copy.wait_send()
+
+
+def work_kernel(
+    plan, own, rdest, state, adj, wts, slp, radj, rwts, rslp, src_adj, wind
+):
+    src_adj[...] = jnp.zeros_like(src_adj)
+    wind[...] = jnp.zeros_like(wind)
+
+    def tile(block, t, row, a_ref, w_ref, s_ref):
+        @pl.when(block >= 0)
+        def _():
+            a = a_ref[t]
+            src_adj[block] += jnp.dot(a, w_ref[t], preferred_element_type=jnp.float32)
+            deriv = lax.dot_general(
+                state[block], s_ref[t], (((1,), (1,)), ((), ())),
+                preferred_element_type=jnp.float32,
+            )
+            wind[row] = jnp.sum(deriv * a.astype(jnp.float32), axis=0, keepdims=True)
+
+    def local(t, _):
+        tile(own[t], t, plan.count * REGION + t, adj, wts, slp)
+        return 0
+
+    lax.fori_loop(0, adj.shape[0], local, 0)
+    for k in range(plan.count):
+
+        def arrived(t, _, k=k):
+            tile(rdest[k, t], plan.bases[k] + t, k * REGION + t, radj, rwts, rslp)
+            return 0
+
+        lax.fori_loop(0, plan.caps[k], arrived, 0)
+
+
+def wind_kernel(plan, mesh, ntile, slot, wind, out, held, ssem, rsem):
+    lat, core = lax.axis_index("lat"), lax.axis_index("lev")
+    held[...] = jnp.zeros_like(held)
+    here = (lax.axis_index("grp"), lax.axis_index("lon"), lat)
+    partner = index_of_axes(mesh, here + (1 - core,))
+    barrier = pltpu.get_barrier_semaphore()
+    pl.semaphore_signal(barrier, inc=1, device_id=partner, device_id_type=MESH)
+    expected = 1
+    for step in plan.near:
+        there = plan.exists(lat, step[0])
+        expected = expected + 2 * there.astype(jnp.int32)
+
+        @pl.when(there)
+        def _(step=step):
+            for c in range(2):
+                pl.semaphore_signal(
+                    barrier, inc=1,
+                    device_id=index_of_axes(mesh, plan.device(step, 1, c)), device_id_type=MESH,
+                )
+
+    pl.semaphore_wait(barrier, expected)
+
+    def back(k, step, c):
+        rows = pl.ds(k * REGION, REGION)
+        to = core if c == 0 else 1 - core
+        return pltpu.make_async_remote_copy(
+            src_ref=wind.at[rows], dst_ref=held.at[core, rows],
+            send_sem=ssem.at[k, c], recv_sem=rsem.at[k, c],
+            device_id=index_of_axes(mesh, plan.device(step, -1, to)), device_id_type=MESH,
+        )
+
+    mine = pl.ds(plan.count * REGION, ntile)
+    across = pltpu.make_async_remote_copy(
+        src_ref=wind.at[mine], dst_ref=held.at[core, mine],
+        send_sem=ssem.at[plan.count, 0], recv_sem=rsem.at[plan.count, 0],
+        device_id=partner, device_id_type=MESH,
+    )
+    for k, step in enumerate(plan.near):
+
+        @pl.when(plan.exists(lat, -step[0]))
+        def _(k=k, step=step):
+            for c in range(2):
+                back(k, step, c).start()
+
+    across.start()
+    held[core, mine] = wind[mine]
+    across.wait()
+    for k, step in enumerate(plan.near):
+
+        @pl.when(plan.exists(lat, step[0]))
+        def _(k=k, step=step):
+            for c in range(2):
+                back(k, step, c).wait_recv()
+
+        @pl.when(plan.exists(lat, -step[0]))
+        def _(k=k, step=step):
+            for c in range(2):
+                back(k, step, c).wait_send()
+
+    for t in range(ntile):
+        out[t] = held[0, slot[t]] + held[1, slot[t]]
+
+
+def on_device(mesh, state, adj_in, weights, slopes, dep_lat, dep_lon):
+    rows, cols, levels, fields, cells = state.shape
+    tpb, points = adj_in.shape[2], adj_in.shape[-1]
+    channels, ntile, half = levels * fields, rows * cols * tpb, points // 2
+    plan = Plan(mesh, ntile)
+    plan.copies = sum(len(c) for c in plan.chunks)
+    f32, bf16, i32 = jnp.float32, jnp.bfloat16, jnp.int32
+    shape = jax.ShapeDtypeStruct
+    anyref = pl.BlockSpec(memory_space=pl.ANY)
+    smem = pl.BlockSpec(memory_space=pltpu.SMEM)
+    vmem = pl.BlockSpec(memory_space=pltpu.VMEM)
+    params = functools.partial(pltpu.CompilerParams, vmem_limit_bytes=48 * 2**20)
+
+    st = state.reshape(rows * cols, channels, cells)
+    adj = adj_in.reshape(ntile, channels, points)
+    wts = weights.reshape(ntile, points, cells)
+    slp = slopes.reshape(ntile, points, cells)
+
+    padj, pwts, pslp, dest, own, slot, over = pl.pallas_call(
+        functools.partial(pack_kernel, plan, (rows, cols, tpb, half)),
+        out_shape=(
+            shape((plan.slots, channels, points), bf16),
+            shape((plan.slots, half, cells), bf16),
+            shape((plan.slots, half, cells), bf16),
+            shape((plan.count, REGION), i32),
+            shape((ntile,), i32),
+            shape((ntile,), i32),
+            shape((1,), i32),
+        ),
+        in_specs=[smem, smem, anyref, anyref, anyref],
+        out_specs=(anyref, anyref, anyref, smem, smem, smem, smem),
+        scratch_shapes=[pltpu.SMEM((plan.count + ntile,), i32), pltpu.SemaphoreType.DMA((ntile, 3))],
+        compiler_params=params(),
+        name="pack",
+    )(dep_lat.reshape(ntile), dep_lon.reshape(ntile), adj, wts, slp)
+
+    any_over = lax.psum(over.astype(f32), mesh.axis_names)[0] > 0
+    tables = jnp.broadcast_to(
+        jnp.pad(dest, ((0, 0), (0, 128 - REGION)))[:, None, :], (plan.count, 8, 128)
+    )
+    groups = plan.copies + plan.count
+    radj, rwts, rslp, rdest = pl.pallas_call(
+        functools.partial(send_kernel, plan, mesh),
+        out_shape=(
+            shape((plan.slots, channels, points), bf16),
+            shape((plan.slots, 2, half, cells), bf16),
+            shape((plan.slots, 2, half, cells), bf16),
+            shape((plan.count, 8, 128), i32),
+        ),
+        in_specs=[anyref] * 4,
+        out_specs=(anyref,) * 4,
+        scratch_shapes=[
+            pltpu.SemaphoreType.DMA((groups, 3)),
+            pltpu.SemaphoreType.DMA((groups, 3)),
+            pltpu.SemaphoreType.DMA((plan.copies, 2)),
+            pltpu.SemaphoreType.DMA((plan.copies, 2)),
+        ],
+        compiler_params=params(collective_id=1, has_side_effects=True),
+        name="send_tiles",
+    )(padj, pwts, pslp, tables)
+
+    lat = lax.axis_index("lat")
+    came = jnp.stack([plan.exists(lat, -a) for a, b in plan.near])
+    rdest = jnp.where(came[:, None], rdest[:, 0, :REGION], -1)
+
+    def owner_path(_):
+        total = (plan.count * REGION) + ntile
+        src_adj, wind = pl.pallas_call(
+            functools.partial(work_kernel, plan),
+            out_shape=(
+                shape((rows * cols, channels, cells), f32),
+                shape((total, 1, points), f32),
+            ),
+            in_specs=[smem, smem] + [vmem] * 7,
+            out_specs=(vmem, vmem),
+            compiler_params=params(),
+            name="tile_products",
+        )(
+            own, rdest, st, adj, wts, slp, radj,
+            rwts.reshape(plan.slots, points, cells), rslp.reshape(plan.slots, points, cells),
+        )
+        wind = pl.pallas_call(
+            functools.partial(wind_kernel, plan, mesh, ntile),
+            out_shape=shape((ntile, 1, points), f32),
+            in_specs=[smem, vmem],
+            out_specs=vmem,
+            scratch_shapes=[
+                pltpu.VMEM((2, total, 1, points), f32),
+                pltpu.SemaphoreType.DMA((plan.count + 1, 2)),
+                pltpu.SemaphoreType.DMA((plan.count + 1, 2)),
+            ],
+            compiler_params=params(collective_id=2, has_side_effects=True),
+            name="wind_rows",
+        )(slot, wind)
+        return src_adj, wind.reshape(ntile, points)
+
+    def general_path(_):
+        return halo_path(state, adj_in, weights, slopes, dep_lat, dep_lon)
+
+    src_adj, wind = lax.cond(any_over, general_path, owner_path, 0)
+    return (
+        src_adj.reshape(rows, cols, levels, fields, cells),
+        wind.reshape(rows, cols, tpb, points),
+    )
 
 
 def solution(mesh):
@@ -78,7 +499,7 @@
         P(("grp", "lat"), "lon", None),
     )
     return jax.shard_map(
-        on_device,
+        functools.partial(on_device, mesh),
         mesh=mesh,
         in_specs=placed,
         out_specs=(

time: 206 us -> 120 us (0.58)
  waiting for transfers between devices: 131 us -> 0 us
  Pallas kernels: 0 us -> 67.6 us
  blocking collectives: 3.09 us -> 42.6 us
  local copies, waits for them, and re-layouts: 31.6 us -> 6.73 us
  other arithmetic: 19.6 us -> 0.07 us
  starting transfers between devices: 15.6 us -> 0 us
  matrix products: 3.49 us -> 0 us
    ppermute x8 -> x0, waiting for transfers between devices: 131 us -> none  [the longest x4 88.7 us: with_halo(): after = lax.ppermute(initial, axis, down)]
    pallas_call x0 -> x4, Pallas kernels: none -> 67.6 us  [the longest x1 48.7 us: on_device(): pl.pallas_call(functools.partial(send_kernel, plan, mesh), out_shape=(sha...]
    psum x1, blocking collectives: 3.09 us -> 42.6 us  [on_device(): any_over = lax.psum(over.astype(f32), mesh.axis_names)[0] > 0]
    ppermute x8 -> x0, starting transfers between devices: 15.6 us -> none  [the longest x4 11.7 us: with_halo(): before = lax.ppermute(last, axis, up)]
    unnamed x18 -> x11, local copies, waits for them, and re-layouts: 13 us -> 2.18 us
    scatter-add x3 -> x0, other arithmetic: 10.5 us -> none  [the longest x1 9.43 us: on_device(): jax.ops.segment_sum(contrib.reshape(ntile, channels * cells), target, num...]
    concatenate x1 -> x0, other arithmetic: 6.17 us -> none  [with_halo(): array = jnp.concatenate([before, array, after], axis=dim)]
    slice x4 -> x0, local copies, waits for them, and re-layouts: 5.68 us -> none  [the longest x1 2.49 us: with_halo(): last = lax.slice_in_dim(array, length - width, length, axis=dim)]
  transfers between devices with their start and end apart: 8 -> 0, of which waited for: 6 -> 0; matrix products, arithmetic and copies ran while one was open for 13% -> 0% of each run, Pallas kernels for 0% -> 0%
where the time goes in v1:
time: 120 us; the launch traced here: 119 us
  Pallas kernels  67.6 us (56%)
  blocking collectives  42.6 us (36%)
  local copies, waits for them, and re-layouts  6.73 us (6%)
  between operations  2.05 us (2%)
    pallas_call x1, Pallas kernels, on_device(): pl.pallas_call(functools.partial(send_kernel, plan, mesh), out_shape=(sha...  48.7 us
    psum x1, blocking collectives, on_device(): any_over = lax.psum(over.astype(f32), mesh.axis_names)[0] > 0  42.6 us
    pallas_call x1, Pallas kernels, owner_path(): pl.pallas_call(functools.partial(work_kernel, plan), out_shape=(shape((ro...  8.83 us
    pallas_call x1, Pallas kernels, owner_path(): pl.pallas_call(functools.partial(wind_kernel, plan, mesh, ntile), out_sha...  6.2 us
    pallas_call x1, Pallas kernels, on_device(): pl.pallas_call(functools.partial(pack_kernel, plan, (rows, cols, tpb, hal...  3.92 us
    reshape x1, local copies, waits for them, and re-layouts, on_device(): src_adj.reshape(rows, cols, levels, fields, cells)  2.7 us

profile of v1, /device:TPU:0, one launch (start us, length us, event | category | flops | bytes accessed | tf_op | source)
XLA Modules:
  0.0 119.3 jit_solution(2706451790744888107)
XLA Ops:
  0.6 0.8 copy.13
  1.4 0.1 reshape.249.dlat
  1.5 0.8 copy.14
  2.3 0.1 reshape.250.dlon
  2.4 3.9 %pack.1 = (bf16[36,192,128]{2,1,0:T(8,128)(2,1)S(1)}, bf16[36,64,256]{2,1,0:T(8,128)(2,1)S(1)}, bf16[36,64,256]{2,1,0:T(8,128)(2,1)S(1)}, s32[5,16]{1,0:T(8,128)...) custom-call(s32[16]{0:T(128)S(1)} %reshape.249.dlat, s32[16]{0:T(128)S(1)} %reshape.250.dlon, ...), custom_call_target="tpu_custom_call" | custom-call | tf_op jit(solution)/shard_map/pack/pallas_call | solution.py:404
  6.3 0.0 copy-start.1
  6.3 0.0 copy-start.2
  6.3 0.0 copy-start.5
  6.3 0.0 copy-start.6
  6.4 48.7 %send_tiles.1 = (bf16[36,192,128]{2,1,0:T(8,128)(2,1)}, bf16[36,2,64,256]{3,2,1,0:T(8,128)(2,1)}, bf16[36,2,64,256]{3,2,1,0:T(8,128)(2,1)}, s32[5,8,128]{2,1,0:T(8,128)S(1)}) custom-call(bf16[36,192,128]{2,1,0:T(8,128)(2,1)S(1)} %get-tuple-element.141.padj, bf16[36,64,256]{2,1,0:T(8,128)(2,1)S(1)} %get-tuple-element.142.pwts, ...), custom_call_target="tpu_custom_call" | custom-call | tf_op jit(solution)/shard_map/send_tiles/pallas_call | solution.py:427
  55.0 0.1 stack.17
  55.8 42.6 %psum.14 = f32[1]{0:T(128)} all-reduce(f32[1]{0:T(128)S(6)} %convert_element_type.12), channel_id=1, replica_groups=mesh['grp'=2,'lon'=2,'lat'=4,'lev'=2] {'grp','lon','lat','lev'}, use_global_device_ids=true, to_apply=%region_0.0 | all-reduce | flops 1 | bytes 8 | tf_op jit(solution)/shard_map/psum | solution.py:422
  99.0 0.0 copy-done.1
  99.1 0.0 copy-done.2
  99.1 0.0 copy-done.5
  99.1 0.0 copy-done.6
  99.1 16.9 %conditional.1 = (f32[8,192,256]{2,1,0:T(8,128)}, f32[2,4,2,128]{3,2,1,0:T(2,128)S(1)}) conditional(s32[]{:T(128)} %bitcast.13, (pred[5]{0:T(512)(128)(4,1)S(1)}, s32[5,8,128]{2,1,0:T(8,128)S(1)}, bf16[2,4,48,4,256]{4,3,2,1,0:T(4,128)(2,1)}, bf16[36,2,64,256]{3,2,1,0:T(8,128)(2,1)}, bf16[36,2,64,256]{3,2,1,0:T(8,128)(2,1)}, ...), branch_computations={%region_1.2_spmd, %region_2.6_spmd} | conditional | flops 411305088 | bytes 193492816 | solution.py:485
  99.1 1.6 %reshape.230.state = bf16[8,192,256]{2,1,0:T(8,128)(2,1)S(1)} reshape(bf16[2,4,48,4,256]{4,3,2,1,0:T(4,128)(2,1)} %get-tuple-element.109) | data formatting | bytes 1572864 | tf_op jit(solution)/shard_map/reshape | solution.py:399
  100.7 0.1 fusion.rdest
  100.8 8.8 %tile_products.1 = (f32[8,192,256]{2,1,0:T(8,128)}, f32[96,1,128]{2,1,0:T(1,128)S(1)}) custom-call(s32[16]{0:T(128)S(1)} %get-tuple-element.106.own, s32[5,16]{1,0:T(8,128)S(1)} %fusion.rdest, bf16[8,192,256]{2,1,0:T(8,128)(2,1)S(1)} %reshape.230.state, bf16[16,192,128]{2,1,0:T(8,128)(2,1)S(1)} %get-tuple-element.110.adj, ...), custom_call_target="tpu_custom_call" | custom-call | tf_op jit(solution)/shard_map/cond/branch_0_fun/tile_products/pallas_call | solution.py:453
  109.6 6.2 %wind_rows.1 = f32[16,1,128]{2,1,0:T(1,128)S(1)} custom-call(s32[16]{0:T(128)S(1)} %get-tuple-element.117.slot, f32[96,1,128]{2,1,0:T(1,128)S(1)} %get-tuple-element.118.wind), custom_call_target="tpu_custom_call" | custom-call | tf_op jit(solution)/shard_map/cond/branch_0_fun/wind_rows/pallas_call | solution.py:467
  116.0 2.7 %reshape.254 = f32[2,4,48,4,256]{4,3,2,1,0:T(4,128)} reshape(f32[8,192,256]{2,1,0:T(8,128)} %get-tuple-element.151) | data formatting | bytes 3145728 | tf_op jit(solution)/shard_map/reshape | solution.py:487
  118.7 0.6 copy.31
  (3 shorter events, 0.0 us)
Async XLA Ops:
  6.3 92.8 %copy-start.1 = (bf16[2,4,2,128,256]{4,3,2,1,0:T(8,128)(2,1)S(1)}, bf16[2,4,2,128,256]{4,3,2,1,0:T(8,128)(2,1)}, u32[]{:S(2)}) copy-start(bf16[2,4,2,128,256]{4,3,2,1,0:T(8,128)(2,1)} %param.22) | copy-start | bytes 3145732
  6.3 92.8 %copy-start.2 = (bf16[2,4,2,48,4,128]{5,4,3,2,1,0:T(4,128)(2,1)S(1)}, bf16[2,4,2,48,4,128]{5,4,3,2,1,0:T(4,128)(2,1)}, u32[]{:S(2)}) copy-start(bf16[2,4,2,48,4,128]{5,4,3,2,1,0:T(4,128)(2,1)} %param.21) | copy-start | bytes 2359300
  6.3 92.8 %copy-start.5 = (s32[2,4,2]{1,2,0:T(2,128)S(1)}, s32[2,4,2]{1,2,0:T(2,128)}, u32[]{:S(2)}) copy-start(s32[2,4,2]{1,2,0:T(2,128)} %param.24) | copy-start | bytes 196
  6.3 92.8 %copy-start.6 = (s32[2,4,2]{1,2,0:T(2,128)S(1)}, s32[2,4,2]{1,2,0:T(2,128)}, u32[]{:S(2)}) copy-start(s32[2,4,2]{1,2,0:T(2,128)} %param.25) | copy-start | bytes 196

commit v2 on v1

--- a/solution.py
+++ b/solution.py
@@ -69,7 +69,7 @@
     )
     summed = summed.reshape(tall, wide, channels, cells)
     owned = fold_lat(fold_lon(summed))
-    return owned.reshape(rows_dev * cols_dev, channels, cells), wind
+    return owned.reshape(rows_dev * cols_dev, levels_dev, fields, cells), wind
 
 
 class Plan:
@@ -79,11 +79,14 @@
         self.near = [(a, b) for b in lons for a in (-1, 1, 0) if (a, b) != (0, 0)]
         self.near.sort(key=lambda d: -(abs(d[0]) + abs(d[1])))
         self.caps, self.bases, self.chunks = [], [], []
+        self.rooms = []
         for a, b in self.near:
-            cap = 5 if a and b else (8 if b else 9)
+            edge, inner = (6, 5) if a and b else ((9, 5) if b else (9, 10))
+            low, cap = min(edge, inner), max(edge, inner)
             self.bases.append(sum(self.caps))
             self.caps.append(cap)
-            self.chunks.append([(0, 4, False), (4, 4, True)] if b and not a else [(0, cap, False)])
+            self.rooms.append((edge, inner))
+            self.chunks.append([(0, low, None), (low, cap - low, edge > inner)])
         self.slots = sum(self.caps)
         self.count = len(self.near)
 
@@ -132,7 +135,8 @@
     def place(t, _):
         r = t // (cols * tpb)
         c = lax.rem(t // tpb, cols)
-        sr, sc = r + dlat[t], c + dlon[t]
+        u = lax.rem(t, tpb)
+        sr, sc = r + dlat[r, c, u], c + dlon[r, c, u]
         a = jnp.where(sr < 0, -1, jnp.where(sr >= rows, 1, 0))
         b = jnp.where(sc < 0, -1, jnp.where(sc >= cols, 1, 0))
         block = (sr - a * rows) * cols + sc - b * cols
@@ -152,9 +156,7 @@
             def _(k=k, x=x, y=y):
                 pos = fill[k]
                 fill[k] = pos + 1
-                room = plan.caps[k]
-                if y and not x:
-                    room = jnp.where(plan.polar(lat), room, 4)
+                room = jnp.where(plan.polar(lat), *plan.rooms[k])
                 fits = pos < room
                 at = jnp.where(fits, pos, 0)
                 slot[t] = k * REGION + at
@@ -188,27 +190,53 @@
 
 
 def send_kernel(
-    plan, mesh, padj, pwts, pslp, pdest, radj, rwts, rslp, rdest, ssem, rsem, fsem, gsem
+    plan, mesh, padj, pwts, pslp, pdest, mine, radj, rwts, rslp, rdest, over,
+    plane, both, quad, ssem, rsem, fsem, gsem, psem, qsem, usem, vsem,
 ):
+    grp, lon = lax.axis_index("grp"), lax.axis_index("lon")
     lat, core = lax.axis_index("lat"), lax.axis_index("lev")
+    ncore = mesh.shape["lev"]
+    nplane, nquad = plan.nlon * plan.nlat, mesh.shape["grp"] * ncore
+    here, corner = lon * plan.nlat + lat, grp * ncore + core
     polar = plan.polar(lat)
-    partner = index_of_axes(
-        mesh, (lax.axis_index("grp"), lax.axis_index("lon"), lat, 1 - core)
-    )
+    partner = index_of_axes(mesh, (grp, lon, lat, 1 - core))
+
+    def in_plane(q):
+        return index_of_axes(mesh, (grp, q // plan.nlat, lax.rem(q, plan.nlat), core))
+
+    def in_quad(q):
+        return index_of_axes(mesh, (q // ncore, lon, lat, lax.rem(q, ncore)))
+
+    def others(count, me, do):
+        def step(q, _):
+            pl.when(q != me)(lambda: do(q))
+            return 0
+
+        lax.fori_loop(0, count, step, 0)
+
     barrier = pltpu.get_barrier_semaphore()
-    expected = 1
-    pl.semaphore_signal(barrier, inc=1, device_id=partner, device_id_type=MESH)
-    for step in plan.near:
-        there = plan.exists(lat, step[0])
-        expected = expected + there.astype(jnp.int32)
-
-        @pl.when(there)
-        def _(step=step):
-            pl.semaphore_signal(
-                barrier, inc=1, device_id=index_of_axes(mesh, plan.device(step)), device_id_type=MESH
-            )
-
-    pl.semaphore_wait(barrier, expected)
+
+    def greet(device):
+        pl.semaphore_signal(barrier, inc=1, device_id=device, device_id_type=MESH)
+
+    others(nplane, here, lambda q: greet(in_plane(q)))
+    others(nquad, corner, lambda q: greet(in_quad(q)))
+    pl.semaphore_wait(barrier, nplane + nquad - 2)
+
+    def flag(src, table, me, to, q, send, recv):
+        return pltpu.make_async_remote_copy(
+            src_ref=src, dst_ref=table.at[me], send_sem=send.at[q], recv_sem=recv.at[me],
+            device_id=to(q), device_id_type=MESH,
+        )
+
+    def flag_in(src, table, to, q, send, recv):
+        return pltpu.make_async_remote_copy(
+            src_ref=src, dst_ref=table.at[q], send_sem=send.at[q], recv_sem=recv.at[q],
+            device_id=to(q), device_id_type=MESH,
+        )
+
+    others(nplane, here, lambda q: flag(mine, plane, here, in_plane, q, psem, qsem).start())
+    plane[here] = mine[...]
 
     def groups():
         n = 0
@@ -216,8 +244,9 @@
             for off, size, far in plan.chunks[k]:
                 rows = pl.ds(plan.bases[k] + off, size)
                 send, get = plan.exists(lat, step[0]), plan.exists(lat, -step[0])
-                if far:
-                    send, get = send & polar, get & polar
+                if far is not None:
+                    send = send & (polar == far)
+                    get = get & (plan.polar(lat - step[0]) == far)
                 yield n, k, step, off, rows, send, get
                 n += 1
 
@@ -259,8 +288,16 @@
         def _():
             if off == 0:
                 table(k, step).start()
-            for copy in outgoing(n, step, rows):
+            for copy in outgoing(n, step, rows)[:2]:
                 copy.start()
+
+    for n, k, step, off, rows, send, get in groups():
+        pl.when(send)(lambda: outgoing(n, step, rows)[2].start())
+
+    others(nplane, here, lambda q: flag_in(mine, plane, in_plane, q, psem, qsem).wait_recv())
+    both[...] = jnp.max(plane[...], axis=0)
+    others(nquad, corner, lambda q: flag(both, quad, corner, in_quad, q, usem, vsem).start())
+    quad[corner] = both[...]
 
     for n, k, step, off, rows, send, get in groups():
 
@@ -270,6 +307,10 @@
             for j in range(2):
                 arrive[j].wait_recv()
                 on[j].start()
+
+    others(nquad, corner, lambda q: flag_in(both, quad, in_quad, q, usem, vsem).wait())
+    others(nplane, here, lambda q: flag_in(mine, plane, in_plane, q, psem, qsem).wait_send())
+    over[0] = jnp.max(quad[...])
 
     for n, k, step, off, rows, send, get in groups():
 
@@ -290,34 +331,62 @@
 
 
 def work_kernel(
-    plan, own, rdest, state, adj, wts, slp, radj, rwts, rslp, src_adj, wind
+    plan, own, rdest, state, adj, wts, slp, radj, rwts, rslp, src_adj, wind,
+    total, adj_in, wts_in, slp_in, sems,
 ):
-    src_adj[...] = jnp.zeros_like(src_adj)
-    wind[...] = jnp.zeros_like(wind)
-
-    def tile(block, t, row, a_ref, w_ref, s_ref):
+    ntile = adj.shape[0]
+
+    def copies(t, at, refs):
+        into = (adj_in, wts_in, slp_in)
+        return [
+            pltpu.make_async_copy(ref.at[t], dst.at[at], sems.at[at, j])
+            for j, (ref, dst) in enumerate(zip(refs, into))
+        ]
+
+    def begin(block, t, at, refs):
         @pl.when(block >= 0)
         def _():
-            a = a_ref[t]
-            src_adj[block] += jnp.dot(a, w_ref[t], preferred_element_type=jnp.float32)
+            for copy in copies(t, at, refs):
+                copy.start()
+
+    def tile(block, t, at, row, refs):
+        @pl.when(block >= 0)
+        def _():
+            for copy in copies(t, at, refs):
+                copy.wait()
+            a = adj_in[at]
+            total[block] += jnp.dot(a, wts_in[at], preferred_element_type=jnp.float32)
             deriv = lax.dot_general(
-                state[block], s_ref[t], (((1,), (1,)), ((), ())),
+                state[block].reshape(total.shape[1:]), slp_in[at], (((1,), (1,)), ((), ())),
                 preferred_element_type=jnp.float32,
             )
             wind[row] = jnp.sum(deriv * a.astype(jnp.float32), axis=0, keepdims=True)
 
-    def local(t, _):
-        tile(own[t], t, plan.count * REGION + t, adj, wts, slp)
+    def every(do):
+        def local(t, _):
+            do(own[t], t, t, plan.count * REGION + t, (adj, wts, slp))
+            return 0
+
+        lax.fori_loop(0, ntile, local, 0)
+        for k in range(plan.count):
+
+            def arrived(i, _, k=k):
+                t = plan.bases[k] + i
+                do(rdest[k, i], t, ntile + t, k * REGION + i, (radj, rwts, rslp))
+                return 0
+
+            lax.fori_loop(0, plan.caps[k], arrived, 0)
+
+    every(lambda block, t, at, row, refs: begin(block, t, at, refs))
+    total[...] = jnp.zeros_like(total)
+    wind[...] = jnp.zeros_like(wind)
+    every(tile)
+
+    def give(b, _):
+        src_adj[b] = total[b].reshape(src_adj.shape[1:])
         return 0
 
-    lax.fori_loop(0, adj.shape[0], local, 0)
-    for k in range(plan.count):
-
-        def arrived(t, _, k=k):
-            tile(rdest[k, t], plan.bases[k] + t, k * REGION + t, radj, rwts, rslp)
-            return 0
-
-        lax.fori_loop(0, plan.caps[k], arrived, 0)
+    lax.fori_loop(0, total.shape[0], give, 0)
 
 
 def wind_kernel(plan, mesh, ntile, slot, wind, out, held, ssem, rsem):
@@ -396,7 +465,7 @@
     vmem = pl.BlockSpec(memory_space=pltpu.VMEM)
     params = functools.partial(pltpu.CompilerParams, vmem_limit_bytes=48 * 2**20)
 
-    st = state.reshape(rows * cols, channels, cells)
+    st = state.reshape(rows * cols, levels, fields, cells)
     adj = adj_in.reshape(ntile, channels, points)
     wts = weights.reshape(ntile, points, cells)
     slp = slopes.reshape(ntile, points, cells)
@@ -417,32 +486,39 @@
         scratch_shapes=[pltpu.SMEM((plan.count + ntile,), i32), pltpu.SemaphoreType.DMA((ntile, 3))],
         compiler_params=params(),
         name="pack",
-    )(dep_lat.reshape(ntile), dep_lon.reshape(ntile), adj, wts, slp)
-
-    any_over = lax.psum(over.astype(f32), mesh.axis_names)[0] > 0
+    )(dep_lat, dep_lon, adj, wts, slp)
+
     tables = jnp.broadcast_to(
         jnp.pad(dest, ((0, 0), (0, 128 - REGION)))[:, None, :], (plan.count, 8, 128)
     )
     groups = plan.copies + plan.count
-    radj, rwts, rslp, rdest = pl.pallas_call(
+    nplane = plan.nlon * plan.nlat
+    nquad = mesh.shape["grp"] * mesh.shape["lev"]
+    dma = pltpu.SemaphoreType.DMA
+    radj, rwts, rslp, rdest, over = pl.pallas_call(
         functools.partial(send_kernel, plan, mesh),
         out_shape=(
             shape((plan.slots, channels, points), bf16),
             shape((plan.slots, 2, half, cells), bf16),
             shape((plan.slots, 2, half, cells), bf16),
             shape((plan.count, 8, 128), i32),
+            shape((1,), i32),
         ),
-        in_specs=[anyref] * 4,
-        out_specs=(anyref,) * 4,
+        in_specs=[anyref] * 4 + [vmem],
+        out_specs=(anyref,) * 4 + (smem,),
         scratch_shapes=[
+            pltpu.VMEM((nplane, 8, 128), i32),
+            pltpu.VMEM((8, 128), i32),
+            pltpu.VMEM((nquad, 8, 128), i32),
             pltpu.SemaphoreType.DMA((groups, 3)),
             pltpu.SemaphoreType.DMA((groups, 3)),
             pltpu.SemaphoreType.DMA((plan.copies, 2)),
             pltpu.SemaphoreType.DMA((plan.copies, 2)),
+            dma((nplane,)), dma((nplane,)), dma((nquad,)), dma((nquad,)),
         ],
         compiler_params=params(collective_id=1, has_side_effects=True),
         name="send_tiles",
-    )(padj, pwts, pslp, tables)
+    )(padj, pwts, pslp, tables, jnp.broadcast_to(over, (8, 128)))
 
     lat = lax.axis_index("lat")
     came = jnp.stack([plan.exists(lat, -a) for a, b in plan.near])
@@ -453,11 +529,18 @@
         src_adj, wind = pl.pallas_call(
             functools.partial(work_kernel, plan),
             out_shape=(
-                shape((rows * cols, channels, cells), f32),
+                shape((rows * cols, levels, fields, cells), f32),
                 shape((total, 1, points), f32),
             ),
-            in_specs=[smem, smem] + [vmem] * 7,
+            in_specs=[smem, smem, vmem] + [anyref] * 6,
             out_specs=(vmem, vmem),
+            scratch_shapes=[
+                pltpu.VMEM((rows * cols, channels, cells), f32),
+                pltpu.VMEM((ntile + plan.slots, channels, points), bf16),
+                pltpu.VMEM((ntile + plan.slots, points, cells), bf16),
+                pltpu.VMEM((ntile + plan.slots, points, cells), bf16),
+                dma((ntile + plan.slots, 3)),
+            ],
             compiler_params=params(),
             name="tile_products",
         )(
@@ -482,7 +565,7 @@
     def general_path(_):
         return halo_path(state, adj_in, weights, slopes, dep_lat, dep_lon)
 
-    src_adj, wind = lax.cond(any_over, general_path, owner_path, 0)
+    src_adj, wind = lax.cond(over[0] > 0, general_path, owner_path, 0)
     return (
         src_adj.reshape(rows, cols, levels, fields, cells),
         wind.reshape(rows, cols, tpb, points),

time: 120 us -> 82.4 us (0.69)
  blocking collectives: 42.6 us -> 0 us
  Pallas kernels: 67.6 us -> 78.1 us
  local copies, waits for them, and re-layouts: 6.73 us -> 2.95 us
    psum x1 -> x0, blocking collectives: 42.6 us -> none  [on_device(): any_over = lax.psum(over.astype(f32), mesh.axis_names)[0] > 0]
    pallas_call x1, Pallas kernels: 48.7 us -> 54.6 us  [on_device(): pl.pallas_call(functools.partial(send_kernel, plan, mesh), out_shape=(sha...]
    reshape x4 -> x0, local copies, waits for them, and re-layouts: 4.43 us -> none  [the longest x1 2.7 us: on_device(): src_adj.reshape(rows, cols, levels, fields, cells)]
    pallas_call x1, Pallas kernels: 6.2 us -> 10.1 us  [owner_path(): pl.pallas_call(functools.partial(wind_kernel, plan, mesh, ntile), out_sha...]
where the time goes in v2:
time: 82.4 us; the launch traced here: 82.7 us
  Pallas kernels  78.1 us (95%)
  local copies, waits for them, and re-layouts  2.95 us (4%)
  between operations  1.32 us (2%)
    pallas_call x1, Pallas kernels, on_device(): pl.pallas_call(functools.partial(send_kernel, plan, mesh), out_shape=(sha...  54.6 us
    pallas_call x1, Pallas kernels, owner_path(): pl.pallas_call(functools.partial(wind_kernel, plan, mesh, ntile), out_sha...  10.1 us
    pallas_call x1, Pallas kernels, owner_path(): pl.pallas_call(functools.partial(work_kernel, plan), out_shape=(shape((ro...  9.21 us
    pallas_call x1, Pallas kernels, on_device(): pl.pallas_call(functools.partial(pack_kernel, plan, (rows, cols, tpb, hal...  4.11 us
    unnamed x13, local copies, waits for them, and re-layouts  2.18 us

profile of v2, /device:TPU:0, one launch (start us, length us, event | category | flops | bytes accessed | tf_op | source)
XLA Modules:
  0.0 82.7 jit_solution(11802199735560551055)
XLA Ops:
  0.6 0.8 copy.13.dlat
  1.4 0.8 copy.14.dlon
  2.2 4.1 %pack.1 = (bf16[41,192,128]{2,1,0:T(8,128)(2,1)S(1)}, bf16[41,64,256]{2,1,0:T(8,128)(2,1)S(1)}, bf16[41,64,256]{2,1,0:T(8,128)(2,1)S(1)}, s32[5,16]{1,0:T(8,128)...) custom-call(s32[2,4,2]{2,1,0:T(4,128)S(1)} %copy.13.dlat, s32[2,4,2]{2,1,0:T(4,128)S(1)} %copy.14.dlon, ...), custom_call_target="tpu_custom_call" | custom-call | tf_op jit(solution)/shard_map/pack/pallas_call | solution.py:473
  6.3 0.6 broadcast_in_dim.30.mine
  7.0 0.0 copy-start.1
  7.0 0.0 copy-start.2
  7.0 0.0 copy-start.3
  7.0 0.0 copy-start.7
  7.0 0.0 copy-start.8
  7.0 54.6 %send_tiles.1 = (bf16[41,192,128]{2,1,0:T(8,128)(2,1)}, bf16[41,2,64,256]{3,2,1,0:T(8,128)(2,1)}, bf16[41,2,64,256]{3,2,1,0:T(8,128)(2,1)}, s32[5,8,128]{2,1,0:T(8,128)S(1)}, s32[1]{0:T(128)}) custom-call(bf16[41,192,128]{2,1,0:T(8,128)(2,1)S(1)} %get-tuple-element.141.padj, bf16[41,64,256]{2,1,0:T(8,128)(2,1)S(1)} %get-tuple-element.142.pwts, ...), custom_call_target="tpu_custom_call" | custom-call | tf_op jit(solution)/shard_map/send_tiles/pallas_call | solution.py:498
  61.7 0.1 stack.17
  62.3 0.0 copy-done.1
  62.3 0.0 copy-done.2
  62.3 0.0 copy-done.3
  62.3 0.0 copy-done.7
  62.4 0.0 copy-done.8
  62.4 19.7 %conditional.1 = (f32[8,48,4,256]{3,2,1,0:T(4,128)}, f32[2,4,2,128]{3,2,1,0:T(2,128)S(1)}) conditional(s32[]{:T(128)} %bitcast.14, (pred[5]{0:T(512)(128)(4,1)S(1)}, s32[5,8,128]{2,1,0:T(8,128)S(1)}, bf16[2,4,48,4,256]{4,3,2,1,0:T(4,128)(2,1)}, bf16[41,2,64,256]{3,2,1,0:T(8,128)(2,1)}, bf16[41,2,64,256]{3,2,1,0:T(8,128)(2,1)}, ...), branch_computations={%region_0.1_spmd, %region_1.5_spmd} | conditional | flops 411305088 | bytes 200832880 | solution.py:568
  62.4 0.1 fusion.rdest
  62.5 9.2 %tile_products.1 = (f32[8,48,4,256]{3,2,1,0:T(4,128)}, f32[96,1,128]{2,1,0:T(1,128)S(1)}) custom-call(s32[16]{0:T(128)S(1)} %get-tuple-element.106.own, s32[5,16]{1,0:T(8,128)S(1)} %fusion.rdest, bf16[8,48,4,256]{3,2,1,0:T(4,128)(2,1)} %bitcast.49, bf16[16,192,128]{2,1,0:T(8,128)(2,1)S(1)} %get-tuple-element.110.adj, ...), custom_call_target="tpu_custom_call" | custom-call | tf_op jit(solution)/shard_map/cond/branch_0_fun/tile_products/pallas_call | solution.py:529
  71.7 10.1 %wind_rows.1 = f32[16,1,128]{2,1,0:T(1,128)S(1)} custom-call(s32[16]{0:T(128)S(1)} %get-tuple-element.117.slot, f32[96,1,128]{2,1,0:T(1,128)S(1)} %get-tuple-element.118.wind), custom_call_target="tpu_custom_call" | custom-call | tf_op jit(solution)/shard_map/cond/branch_0_fun/wind_rows/pallas_call | solution.py:550
  82.1 0.6 copy.31
  (3 shorter events, 0.0 us)
Async XLA Ops:
  7.0 55.3 %copy-start.1 = (bf16[2,4,2,128,256]{4,3,2,1,0:T(8,128)(2,1)S(1)}, bf16[2,4,2,128,256]{4,3,2,1,0:T(8,128)(2,1)}, u32[]{:S(2)}) copy-start(bf16[2,4,2,128,256]{4,3,2,1,0:T(8,128)(2,1)} %param.22) | copy-start | bytes 3145732
  7.0 55.3 %copy-start.2 = (bf16[2,4,2,48,4,128]{5,4,3,2,1,0:T(4,128)(2,1)S(1)}, bf16[2,4,2,48,4,128]{5,4,3,2,1,0:T(4,128)(2,1)}, u32[]{:S(2)}) copy-start(bf16[2,4,2,48,4,128]{5,4,3,2,1,0:T(4,128)(2,1)} %param.21) | copy-start | bytes 2359300
  7.0 55.3 %copy-start.3 = (bf16[2,4,2,128,256]{4,3,2,1,0:T(8,128)(2,1)S(1)}, bf16[2,4,2,128,256]{4,3,2,1,0:T(8,128)(2,1)}, u32[]{:S(2)}) copy-start(bf16[2,4,2,128,256]{4,3,2,1,0:T(8,128)(2,1)} %param.23) | copy-start | bytes 3145732
  7.0 55.3 %copy-start.7 = (s32[2,4,2]{1,2,0:T(2,128)S(1)}, s32[2,4,2]{1,2,0:T(2,128)}, u32[]{:S(2)}) copy-start(s32[2,4,2]{1,2,0:T(2,128)} %param.24) | copy-start | bytes 196
  7.0 55.3 %copy-start.8 = (s32[2,4,2]{1,2,0:T(2,128)S(1)}, s32[2,4,2]{1,2,0:T(2,128)}, u32[]{:S(2)}) copy-start(s32[2,4,2]{1,2,0:T(2,128)} %param.25) | copy-start | bytes 196

commit v3 on v2

--- a/solution.py
+++ b/solution.py
@@ -113,14 +113,14 @@
 
 
 def pack_kernel(
-    plan, dims, dlat, dlon, adj, wts, slp, padj, pwts, pslp, dest, own, slot, over, fill, sems
+    plan, dims, moved, adj, wts, slp, padj, pwts, pslp, dest, own, slot, mine, over, fill, sems
 ):
     rows, cols, tpb, half = dims
     lat, core = lax.axis_index("lat"), lax.axis_index("lev")
     for k in range(plan.count):
         fill[k] = 0
-        for s in range(REGION):
-            dest[k, s] = -1
+        for s in range(REGION + 1):
+            dest[k, s] = 0
     over[0] = 0
     ntile = rows * cols * tpb
 
@@ -136,7 +136,8 @@
         r = t // (cols * tpb)
         c = lax.rem(t // tpb, cols)
         u = lax.rem(t, tpb)
-        sr, sc = r + dlat[r, c, u], c + dlon[r, c, u]
+        code = moved[r, c, u]
+        sr, sc = r + code // 8 - HW, c + lax.rem(code, 8) - HW
         a = jnp.where(sr < 0, -1, jnp.where(sr >= rows, 1, 0))
         b = jnp.where(sc < 0, -1, jnp.where(sc >= cols, 1, 0))
         block = (sr - a * rows) * cols + sc - b * cols
@@ -165,6 +166,7 @@
                 @pl.when(fits)
                 def _():
                     dest[k, at] = block
+                    dest[k, REGION] = at + 1
                     for copy in copies(t, plan.bases[k] + at):
                         copy.start()
 
@@ -187,11 +189,13 @@
         return 0
 
     lax.fori_loop(0, ntile, finish, 0)
+    mine[...] = jnp.full(mine.shape, over[0], jnp.int32)
 
 
 def send_kernel(
-    plan, mesh, padj, pwts, pslp, pdest, mine, radj, rwts, rslp, rdest, over,
-    plane, both, quad, ssem, rsem, fsem, gsem, psem, qsem, usem, vsem,
+    plan, mesh, padj, pwts, pslp, pdest, mine, own, state, adj, wts, slp,
+    radj, rwts, rslp, rdest, over, home, wind,
+    st_in, adj_in, wts_in, slp_in, total, lsem, plane, both, quad, ssem, rsem, fsem, gsem, psem, qsem, usem, vsem,
 ):
     grp, lon = lax.axis_index("grp"), lax.axis_index("lon")
     lat, core = lax.axis_index("lat"), lax.axis_index("lev")
@@ -214,6 +218,14 @@
 
         lax.fori_loop(0, count, step, 0)
 
+    loads = [
+        pltpu.make_async_copy(src, dst, lsem.at[j])
+        for j, (src, dst) in enumerate(
+            ((state, st_in), (adj, adj_in), (wts, wts_in), (slp, slp_in))
+        )
+    ]
+    for load in loads:
+        load.start()
     barrier = pltpu.get_barrier_semaphore()
 
     def greet(device):
@@ -299,6 +311,27 @@
     others(nquad, corner, lambda q: flag(both, quad, corner, in_quad, q, usem, vsem).start())
     quad[corner] = both[...]
 
+    total[...] = jnp.zeros_like(total)
+    for load in loads:
+        load.wait()
+
+    def local(t, _):
+        a, block = adj_in[t], own[t]
+        contrib = jnp.dot(a, wts_in[t], preferred_element_type=jnp.float32)
+        for b in range(total.shape[0]):
+            total[b] += jnp.where(block == b, contrib, 0.0)
+        deriv = lax.dot_general(
+            st_in[jnp.maximum(block, 0)].reshape(total.shape[1:]), slp_in[t],
+            (((1,), (1,)), ((), ())), preferred_element_type=jnp.float32,
+        )
+        row = jnp.sum(deriv * a.astype(jnp.float32), axis=0, keepdims=True)
+        wind[t] = jnp.where(block >= 0, row, 0.0)
+        return 0
+
+    lax.fori_loop(0, adj_in.shape[0], local, 0)
+    store = pltpu.make_async_copy(total, home, lsem.at[len(loads)])
+    store.start()
+
     for n, k, step, off, rows, send, get in groups():
 
         @pl.when(get)
@@ -311,6 +344,7 @@
     others(nquad, corner, lambda q: flag_in(both, quad, in_quad, q, usem, vsem).wait())
     others(nplane, here, lambda q: flag_in(mine, plane, in_plane, q, psem, qsem).wait_send())
     over[0] = jnp.max(quad[...])
+    store.wait()
 
     for n, k, step, off, rows, send, get in groups():
 
@@ -331,55 +365,48 @@
 
 
 def work_kernel(
-    plan, own, rdest, state, adj, wts, slp, radj, rwts, rslp, src_adj, wind,
-    total, adj_in, wts_in, slp_in, sems,
+    plan, rdest, state, home, radj, rwts, rslp, src_adj, wind,
+    total, adj_in, wts_in, slp_in, sems, hsem,
 ):
-    ntile = adj.shape[0]
-
-    def copies(t, at, refs):
-        into = (adj_in, wts_in, slp_in)
+    lat = lax.axis_index("lat")
+    base = pltpu.make_async_copy(home, total, hsem.at[0])
+
+    def copies(t):
+        pairs = ((radj, adj_in), (rwts, wts_in), (rslp, slp_in))
         return [
-            pltpu.make_async_copy(ref.at[t], dst.at[at], sems.at[at, j])
-            for j, (ref, dst) in enumerate(zip(refs, into))
+            pltpu.make_async_copy(src.at[t], dst.at[t], sems.at[t, j])
+            for j, (src, dst) in enumerate(pairs)
         ]
 
-    def begin(block, t, at, refs):
-        @pl.when(block >= 0)
-        def _():
-            for copy in copies(t, at, refs):
-                copy.start()
-
-    def tile(block, t, at, row, refs):
-        @pl.when(block >= 0)
-        def _():
-            for copy in copies(t, at, refs):
-                copy.wait()
-            a = adj_in[at]
-            total[block] += jnp.dot(a, wts_in[at], preferred_element_type=jnp.float32)
-            deriv = lax.dot_general(
-                state[block].reshape(total.shape[1:]), slp_in[at], (((1,), (1,)), ((), ())),
-                preferred_element_type=jnp.float32,
-            )
-            wind[row] = jnp.sum(deriv * a.astype(jnp.float32), axis=0, keepdims=True)
-
     def every(do):
-        def local(t, _):
-            do(own[t], t, t, plan.count * REGION + t, (adj, wts, slp))
-            return 0
-
-        lax.fori_loop(0, ntile, local, 0)
-        for k in range(plan.count):
+        for k, step in enumerate(plan.near):
+            came = jnp.where(plan.exists(lat, -step[0]), rdest[k, REGION], 0)
 
             def arrived(i, _, k=k):
-                t = plan.bases[k] + i
-                do(rdest[k, i], t, ntile + t, k * REGION + i, (radj, rwts, rslp))
+                do(rdest[k, i], plan.bases[k] + i, k * REGION + i)
                 return 0
 
-            lax.fori_loop(0, plan.caps[k], arrived, 0)
-
-    every(lambda block, t, at, row, refs: begin(block, t, at, refs))
-    total[...] = jnp.zeros_like(total)
+            lax.fori_loop(0, came, arrived, 0)
+
+    def begin(block, t, row):
+        for copy in copies(t):
+            copy.start()
+
+    def tile(block, t, row):
+        for copy in copies(t):
+            copy.wait()
+        a = adj_in[t]
+        total[block] += jnp.dot(a, wts_in[t], preferred_element_type=jnp.float32)
+        deriv = lax.dot_general(
+            state[block].reshape(total.shape[1:]), slp_in[t], (((1,), (1,)), ((), ())),
+            preferred_element_type=jnp.float32,
+        )
+        wind[row] = jnp.sum(deriv * a.astype(jnp.float32), axis=0, keepdims=True)
+
+    base.start()
+    every(begin)
     wind[...] = jnp.zeros_like(wind)
+    base.wait()
     every(tile)
 
     def give(b, _):
@@ -389,7 +416,7 @@
     lax.fori_loop(0, total.shape[0], give, 0)
 
 
-def wind_kernel(plan, mesh, ntile, slot, wind, out, held, ssem, rsem):
+def wind_kernel(plan, mesh, ntile, slot, wind, own_wind, out, held, ssem, rsem):
     lat, core = lax.axis_index("lat"), lax.axis_index("lev")
     held[...] = jnp.zeros_like(held)
     here = (lax.axis_index("grp"), lax.axis_index("lon"), lat)
@@ -422,7 +449,7 @@
 
     mine = pl.ds(plan.count * REGION, ntile)
     across = pltpu.make_async_remote_copy(
-        src_ref=wind.at[mine], dst_ref=held.at[core, mine],
+        src_ref=own_wind, dst_ref=held.at[core, mine],
         send_sem=ssem.at[plan.count, 0], recv_sem=rsem.at[plan.count, 0],
         device_id=partner, device_id_type=MESH,
     )
@@ -434,7 +461,7 @@
                 back(k, step, c).start()
 
     across.start()
-    held[core, mine] = wind[mine]
+    held[core, mine] = own_wind[...]
     across.wait()
     for k, step in enumerate(plan.near):
 
@@ -470,32 +497,32 @@
     wts = weights.reshape(ntile, points, cells)
     slp = slopes.reshape(ntile, points, cells)
 
-    padj, pwts, pslp, dest, own, slot, over = pl.pallas_call(
+    padj, pwts, pslp, dest, own, slot, mine = pl.pallas_call(
         functools.partial(pack_kernel, plan, (rows, cols, tpb, half)),
         out_shape=(
             shape((plan.slots, channels, points), bf16),
             shape((plan.slots, half, cells), bf16),
             shape((plan.slots, half, cells), bf16),
-            shape((plan.count, REGION), i32),
+            shape((plan.count, REGION + 1), i32),
             shape((ntile,), i32),
             shape((ntile,), i32),
-            shape((1,), i32),
+            shape((8, 128), i32),
         ),
-        in_specs=[smem, smem, anyref, anyref, anyref],
-        out_specs=(anyref, anyref, anyref, smem, smem, smem, smem),
-        scratch_shapes=[pltpu.SMEM((plan.count + ntile,), i32), pltpu.SemaphoreType.DMA((ntile, 3))],
+        in_specs=[smem, anyref, anyref, anyref],
+        out_specs=(anyref, anyref, anyref, smem, smem, smem, vmem),
+        scratch_shapes=[pltpu.SMEM((1,), i32), pltpu.SMEM((plan.count + ntile,), i32), pltpu.SemaphoreType.DMA((ntile, 3))],
         compiler_params=params(),
         name="pack",
-    )(dep_lat, dep_lon, adj, wts, slp)
+    )((dep_lat + HW) * 8 + dep_lon + HW, adj, wts, slp)
 
     tables = jnp.broadcast_to(
-        jnp.pad(dest, ((0, 0), (0, 128 - REGION)))[:, None, :], (plan.count, 8, 128)
+        jnp.pad(dest, ((0, 0), (0, 127 - REGION)))[:, None, :], (plan.count, 8, 128)
     )
     groups = plan.copies + plan.count
     nplane = plan.nlon * plan.nlat
     nquad = mesh.shape["grp"] * mesh.shape["lev"]
     dma = pltpu.SemaphoreType.DMA
-    radj, rwts, rslp, rdest, over = pl.pallas_call(
+    radj, rwts, rslp, rdest, over, home, own_wind = pl.pallas_call(
         functools.partial(send_kernel, plan, mesh),
         out_shape=(
             shape((plan.slots, channels, points), bf16),
@@ -503,10 +530,18 @@
             shape((plan.slots, 2, half, cells), bf16),
             shape((plan.count, 8, 128), i32),
             shape((1,), i32),
+            shape((rows * cols, channels, cells), f32),
+            shape((ntile, 1, points), f32),
         ),
-        in_specs=[anyref] * 4 + [vmem],
-        out_specs=(anyref,) * 4 + (smem,),
+        in_specs=[anyref] * 4 + [vmem, smem] + [anyref] * 4,
+        out_specs=(anyref,) * 4 + (smem, anyref, vmem),
         scratch_shapes=[
+            pltpu.VMEM(st.shape, bf16),
+            pltpu.VMEM(adj.shape, bf16),
+            pltpu.VMEM(wts.shape, bf16),
+            pltpu.VMEM(slp.shape, bf16),
+            pltpu.VMEM((rows * cols, channels, cells), f32),
+            dma((5,)),
             pltpu.VMEM((nplane, 8, 128), i32),
             pltpu.VMEM((8, 128), i32),
             pltpu.VMEM((nquad, 8, 128), i32),
@@ -518,48 +553,47 @@
         ],
         compiler_params=params(collective_id=1, has_side_effects=True),
         name="send_tiles",
-    )(padj, pwts, pslp, tables, jnp.broadcast_to(over, (8, 128)))
-
-    lat = lax.axis_index("lat")
-    came = jnp.stack([plan.exists(lat, -a) for a, b in plan.near])
-    rdest = jnp.where(came[:, None], rdest[:, 0, :REGION], -1)
+    )(padj, pwts, pslp, tables, mine, own, st, adj, wts, slp)
+
+    rdest = rdest[:, 0, : REGION + 1]
 
     def owner_path(_):
-        total = (plan.count * REGION) + ntile
+        total = plan.count * REGION
         src_adj, wind = pl.pallas_call(
             functools.partial(work_kernel, plan),
             out_shape=(
                 shape((rows * cols, levels, fields, cells), f32),
                 shape((total, 1, points), f32),
             ),
-            in_specs=[smem, smem, vmem] + [anyref] * 6,
+            in_specs=[smem, vmem] + [anyref] * 4,
             out_specs=(vmem, vmem),
             scratch_shapes=[
                 pltpu.VMEM((rows * cols, channels, cells), f32),
-                pltpu.VMEM((ntile + plan.slots, channels, points), bf16),
-                pltpu.VMEM((ntile + plan.slots, points, cells), bf16),
-                pltpu.VMEM((ntile + plan.slots, points, cells), bf16),
-                dma((ntile + plan.slots, 3)),
+                pltpu.VMEM((plan.slots, channels, points), bf16),
+                pltpu.VMEM((plan.slots, points, cells), bf16),
+                pltpu.VMEM((plan.slots, points, cells), bf16),
+                dma((plan.slots, 3)),
+                dma((1,)),
             ],
             compiler_params=params(),
             name="tile_products",
         )(
-            own, rdest, st, adj, wts, slp, radj,
+            rdest, st, home, radj,
             rwts.reshape(plan.slots, points, cells), rslp.reshape(plan.slots, points, cells),
         )
         wind = pl.pallas_call(
             functools.partial(wind_kernel, plan, mesh, ntile),
             out_shape=shape((ntile, 1, points), f32),
-            in_specs=[smem, vmem],
+            in_specs=[smem, vmem, vmem],
             out_specs=vmem,
             scratch_shapes=[
-                pltpu.VMEM((2, total, 1, points), f32),
+                pltpu.VMEM((2, total + ntile, 1, points), f32),
                 pltpu.SemaphoreType.DMA((plan.count + 1, 2)),
                 pltpu.SemaphoreType.DMA((plan.count + 1, 2)),
             ],
             compiler_params=params(collective_id=2, has_side_effects=True),
             name="wind_rows",
-        )(slot, wind)
+        )(slot, wind, own_wind)
         return src_adj, wind.reshape(ntile, points)
 
     def general_path(_):

time: 82.4 us -> 79.9 us (0.970)
  Pallas kernels: 78.1 us -> 75.6 us
    pallas_call x1, Pallas kernels: 10.1 us -> 8.26 us  [owner_path(): pl.pallas_call(functools.partial(wind_kernel, plan, mesh, ntile), out_sha...]
    pallas_call x1, Pallas kernels: 9.21 us -> 7.83 us  [owner_path(): pl.pallas_call(functools.partial(work_kernel, plan), out_shape=(shape((ro...]
where the time goes in v3:
time: 79.9 us; the launch traced here: 79.7 us
  Pallas kernels  75.6 us (95%)
  local copies, waits for them, and re-layouts  2.35 us (3%)
  between operations  1.44 us (2%)
    pallas_call x1, Pallas kernels, on_device(): pl.pallas_call(functools.partial(send_kernel, plan, mesh), out_shape=(sha...  55.3 us
    pallas_call x1, Pallas kernels, owner_path(): pl.pallas_call(functools.partial(wind_kernel, plan, mesh, ntile), out_sha...  8.26 us
    pallas_call x1, Pallas kernels, owner_path(): pl.pallas_call(functools.partial(work_kernel, plan), out_shape=(shape((ro...  7.83 us
    pallas_call x1, Pallas kernels, on_device(): pl.pallas_call(functools.partial(pack_kernel, plan, (rows, cols, tpb, hal...  4.24 us
    unnamed x13, local copies, waits for them, and re-layouts  2.33 us

profile of v3, /device:TPU:0, one launch (start us, length us, event | category | flops | bytes accessed | tf_op | source)
XLA Modules:
  0.0 79.7 jit_solution(6212720877322678939)
XLA Ops:
  0.6 0.0 copy-start.1
  0.6 0.0 copy-start.5
  0.7 0.0 copy-start.2
  0.7 0.9 %copy.13 = s32[2,4,2]{2,1,0:T(4,128)S(1)} copy(s32[2,4,2]{1,2,0:T(2,128)} %param.24) | data formatting | bytes 128 | tf_op args[4]
  1.6 0.8 copy.14
  2.4 4.2 %pack.1 = (bf16[41,192,128]{2,1,0:T(8,128)(2,1)S(1)}, bf16[41,64,256]{2,1,0:T(8,128)(2,1)S(1)}, bf16[41,64,256]{2,1,0:T(8,128)(2,1)S(1)}, s32[5,17]{1,0:T(8,128)...) custom-call(s32[2,4,2]{2,1,0:T(4,128)S(1)} %add_add_fusion.1.moved, bf16[16,192,128]{2,1,0:T(8,128)(2,1)} %bitcast.35, ...), custom_call_target="tpu_custom_call" | custom-call | tf_op jit(solution)/shard_map/pack/pallas_call | solution.py:500
  6.6 0.0 copy-done.1
  6.7 0.0 copy-done.5
  6.7 0.0 copy-done.2
  6.7 0.0 copy-start.8
  6.7 0.0 copy-start.9
  6.7 55.3 %send_tiles.1 = (bf16[41,192,128]{2,1,0:T(8,128)(2,1)S(1)}, bf16[41,2,64,256]{3,2,1,0:T(8,128)(2,1)S(1)}, bf16[41,2,64,256]{3,2,1,0:T(8,128)(2,1)S(1)}, s32[5,8,...) custom-call(bf16[41,192,128]{2,1,0:T(8,128)(2,1)S(1)} %get-tuple-element.129.padj, ...), custom_call_target="tpu_custom_call" | custom-call | tf_op jit(solution)/shard_map/send_tiles/pallas_call | solution.py:525
  62.7 0.0 copy-done.8
  62.7 0.0 copy-done.9
  62.7 16.4 %conditional.1 = (f32[8,48,4,256]{3,2,1,0:T(4,128)}, f32[2,4,2,128]{3,2,1,0:T(2,128)S(1)}) conditional(s32[]{:T(128)} %bitcast.13, (s32[5,8,128]{2,1,0:T(8,128)S(1)}, bf16[41,2,64,256]{3,2,1,0:T(8,128)(2,1)S(1)}, bf16[41,2,64,256]{3,2,1,0:T(8,128)(2,1)S(1)}, bf16[8,48,4,256]{3,2,1,0:T(4,128)(2,1)}, f32[8,192,256]{2,1,0:T(8,128)}, ...), branch_computations={%region_0.1_spmd, %region_1.5_spmd} | conditional | flops 411305088 | bytes 203978640 | solution.py:602
  62.8 7.8 %tile_products.1 = (f32[8,48,4,256]{3,2,1,0:T(4,128)}, f32[80,1,128]{2,1,0:T(1,128)S(1)}) custom-call(s32[5,17]{1,0:T(8,128)S(1)} %slice_bitcast_fusion.rdest, bf16[8,48,4,256]{3,2,1,0:T(4,128)(2,1)} %get-tuple-element.96.state, f32[8,192,256]{2,1,0:T(8,128)} %get-tuple-element.97.home, bf16[41,192,128]{2,1,0:T(8,128)(2,1)S(1)} %get-tuple-element.98.radj, ...), custom_call_target="tpu_custom_call" | custom-call | tf_op jit(solution)/shard_map/cond/branch_0_fun/tile_products/pallas_call | solution.py:562
  70.6 8.3 %wind_rows.1 = f32[16,1,128]{2,1,0:T(1,128)S(1)} custom-call(s32[16]{0:T(128)S(1)} %get-tuple-element.102.slot, f32[80,1,128]{2,1,0:T(1,128)S(1)} %get-tuple-element.103.wind, f32[16,1,128]{2,1,0:T(1,128)S(1)} %get-tuple-element.104.own_wind), custom_call_target="tpu_custom_call" | custom-call | tf_op jit(solution)/shard_map/cond/branch_0_fun/wind_rows/pallas_call | solution.py:584
  79.1 0.6 copy.31
  (5 shorter events, 0.0 us)
Async XLA Ops:
  0.6 6.0 %copy-start.1 = (bf16[2,4,2,128,256]{4,3,2,1,0:T(8,128)(2,1)S(1)}, bf16[2,4,2,128,256]{4,3,2,1,0:T(8,128)(2,1)}, u32[]{:S(2)}) copy-start(bf16[2,4,2,128,256]{4,3,2,1,0:T(8,128)(2,1)} %param.22) | copy-start | bytes 3145732
  0.6 6.0 %copy-start.5 = (bf16[2,4,2,128,256]{4,3,2,1,0:T(8,128)(2,1)S(1)}, bf16[2,4,2,128,256]{4,3,2,1,0:T(8,128)(2,1)}, u32[]{:S(2)}) copy-start(bf16[2,4,2,128,256]{4,3,2,1,0:T(8,128)(2,1)} %param.23) | copy-start | bytes 3145732
  0.7 6.0 %copy-start.2 = (bf16[2,4,2,48,4,128]{5,4,3,2,1,0:T(4,128)(2,1)S(1)}, bf16[2,4,2,48,4,128]{5,4,3,2,1,0:T(4,128)(2,1)}, u32[]{:S(2)}) copy-start(bf16[2,4,2,48,4,128]{5,4,3,2,1,0:T(4,128)(2,1)} %param.21) | copy-start | bytes 2359300
  6.7 56.0 %copy-start.8 = (s32[2,4,2]{1,2,0:T(2,128)S(1)}, s32[2,4,2]{1,2,0:T(2,128)}, u32[]{:S(2)}) copy-start(s32[2,4,2]{1,2,0:T(2,128)} %param.25) | copy-start | bytes 196
  6.7 56.0 %copy-start.9 = (s32[2,4,2]{1,2,0:T(2,128)S(1)}, s32[2,4,2]{1,2,0:T(2,128)}, u32[]{:S(2)}) copy-start(s32[2,4,2]{1,2,0:T(2,128)} %param.24) | copy-start | bytes 196
